TPU v7x, 32 devices: a whole 2x2x4 slice. The times are simulated.
32 devices in a mesh: groups: 2 (over x), tok: 16 (over z, y, core).
Axes of the slice: x: 2, y: 2, z: 4, core: 2. Of those that a mesh axis runs over, the one named last changes fastest.
Arguments:
- taps: bfloat16 [512, 12288], P('groups', 'tok'), parts along dimension 0, may hold values from -6 to 6
- w_join: bfloat16 [12288, 4096], P('tok'), may hold values from -0.0546875 to 0.0546875
- w_down: bfloat16 [4096, 64], replicated, may hold values from -0.09375 to 0.09375
- w_up: bfloat16 [64, 4096], replicated, may hold values from -0.75 to 0.75
- upstream: bfloat16 [512, 12288], P(('groups', 'tok')), parts along dimension 0, may hold values from -6 to 6
Outputs:
- drafts: bfloat16 [512, 12288], P(('groups', 'tok')), parts along dimension 0
- join_grad: float32 [12288, 8192], P('tok', 'groups'), parts along dimension 1
- down_grad: float32 [8192, 64], P('groups'), parts along dimension 0
- up_grad: float32 [128, 4096], P('groups'), parts along dimension 0
There are 2 independent parts, one for each index of `groups`. A program takes and returns all parts, laid end to end along the dimension named above; an argument that names none is the same for every part. Nothing has to cross between parts.
All inputs are finite; a program needn't handle non-finite values.
Results may differ from a plain program's by a relative error of at most 0.008.
Values may be sent and summed in bfloat16 or wider, within the bound.
A program may use at most 128 MiB of HBM per device.

v0:
```python
import jax
import jax.numpy as jnp
from jax import lax
from jax.sharding import PartitionSpec as P

STEPS = 3


def drafter(joined, w_down, w_up, upstream):
    out_width = w_up.shape[1]
    state = joined.astype(jnp.float32)
    saved = []
    outputs = []
    for section_index in range(STEPS):
        inv_norm = lax.rsqrt(jnp.mean(state * state, axis=-1, keepdims=True) + 1e-06)
        normed = (state * inv_norm).astype(jnp.bfloat16)
        low_rows = jnp.dot(normed, w_down, preferred_element_type=jnp.float32).astype(jnp.bfloat16)
        pre_act = jnp.dot(low_rows, w_up, preferred_element_type=jnp.float32)
        saved.append((state, inv_norm, normed, low_rows, pre_act))
        state = state + jax.nn.silu(pre_act)
        outputs.append(state.astype(jnp.bfloat16))
    drafts = jnp.concatenate(outputs, axis=1)
    state_grad = jnp.zeros(state.shape, jnp.float32)
    down_grad = jnp.zeros(w_down.shape, jnp.float32)
    up_grad = jnp.zeros(w_up.shape, jnp.float32)
    for section_index in reversed(range(STEPS)):
        prior, inv_norm, normed, low_rows, pre_act = saved[section_index]
        block = upstream[:, section_index * out_width : (section_index + 1) * out_width]
        state_grad = state_grad + block.astype(jnp.float32)
        sigma = jax.nn.sigmoid(pre_act)
        act_grad = (state_grad * sigma * (1.0 + pre_act * (1.0 - sigma))).astype(jnp.bfloat16)
        up_grad = up_grad + lax.dot_general(
            low_rows, act_grad, (((0,), (0,)), ((), ())), preferred_element_type=jnp.float32
        )
        low_cot = lax.dot_general(
            act_grad, w_up, (((1,), (1,)), ((), ())), preferred_element_type=jnp.float32
        ).astype(jnp.bfloat16)
        down_grad = down_grad + lax.dot_general(
            normed, low_cot, (((0,), (0,)), ((), ())), preferred_element_type=jnp.float32
        )
        back_grad = lax.dot_general(
            low_cot, w_down, (((1,), (1,)), ((), ())), preferred_element_type=jnp.float32
        )
        inner = jnp.mean(back_grad * prior, axis=-1, keepdims=True)
        state_grad = (
            state_grad + back_grad * inv_norm - prior * inv_norm * inv_norm * inv_norm * inner
        )
    return (drafts, state_grad.astype(jnp.bfloat16), down_grad, up_grad)


def local(taps, w_join, w_down, w_up, upstream):
    tap_rows = taps
    joined = lax.psum_scatter(
        jnp.dot(tap_rows, w_join, preferred_element_type=jnp.float32),
        "tok",
        scatter_dimension=0,
        tiled=True,
    ).astype(jnp.bfloat16)
    drafts, joined_cot, down_part, up_part = drafter(joined, w_down, w_up, upstream)
    tap_rows = taps
    join_grad = lax.dot_general(
        tap_rows,
        lax.all_gather(joined_cot, "tok", axis=0, tiled=True),
        (((0,), (0,)), ((), ())),
        preferred_element_type=jnp.float32,
    )
    down_grad, up_grad = lax.psum((down_part, up_part), "tok")
    return (drafts, join_grad, down_grad, up_grad)


def solution(mesh):
    in_specs = (P("groups", "tok"), P("tok", None), P(), P(), P(("groups", "tok"), None))
    out_specs = (
        P(("groups", "tok"), None),
        P("tok", "groups"),
        P("groups", None),
        P("groups", None),
    )
    return jax.shard_map(local, mesh=mesh, in_specs=in_specs, out_specs=out_specs, check_vma=False)
```

profile of v0, /device:TPU:0, one launch (start us, length us, event | category | flops | bytes accessed | tf_op | source)
XLA Modules:
  0.0 248.5 jit_solution(15311890685420441488)
XLA Ops:
  7.2 6.8 %fusion.21 = f32[256,4096]{1,0:T(8,128)} fusion(bf16[256,768]{1,0:T(8,128)(2,1)} %param.5, bf16[768,4096]{1,0:T(8,128)(2,1)} %param.6), kind=kOutput, calls=%fused_computation.54 | convolution fusion | flops 1610612736 | bytes 10878976 | tf_op jit(solution)/shard_map/dot_general | solution.py:54
  14.1 75.2 %reduce-scatter.2.cloned.1.call-done = f32[16,4096]{1,0:T(8,128)} async-done(((f32[256,4096]{1,0:T(8,128)}), f32[16,4096]{1,0:T(8,128)}) %reduce-scatter.2.cloned.1.call-update) | async-done | bytes 262160 | tf_op jit(solution)/shard_map/reduce_scatter | solution.py:53
  89.4 1.1 fusion.10
  90.5 0.3 convolution_convert_fusion.5
  91.2 0.3 convolution_convert_fusion.4
  91.9 0.3 convolution_convert_fusion.3
  92.6 0.3 multiply_reduce_fusion.1
  93.0 0.3 multiply_convert_fusion.1
  93.5 0.3 multiply_reduce_fusion
  94.3 0.3 fusion.11
  94.6 0.8 fusion.5
  95.5 0.3 fusion.14
  95.8 0.3 fusion.15
  96.2 0.3 convolution_add_fusion.1
  96.5 1.3 convolution_add_fusion
  97.8 0.3 convolution_add_fusion.3
  98.1 1.3 convolution_add_fusion.2
  99.4 0.8 pad_maximum_fusion
  100.2 35.7 %all-gather.2.cloned.1.call-done = bf16[256,4096]{1,0:T(8,128)(2,1)} async-done(((bf16[16,4096]{1,0:T(8,128)(2,1)}), bf16[256,4096]{1,0:T(8,128)(2,1)}) %all-gather.2.cloned.1.call-update) | async-done | bytes 2097168 | tf_op jit(solution)/shard_map/all_gather | solution.py:63
  136.0 8.0 %convolution_bitcast_fusion = f32[768,4096]{0,1:T(8,128)} fusion(bf16[256,4096]{1,0:T(8,128)(2,1)} %all-gather.2.cloned.1.call-done, bf16[256,768]{1,0:T(8,128)(2,1)S(1)} %copy-done.2), kind=kOutput, calls=%fused_computation | convolution fusion | flops 1610612736 | bytes 15073280 | tf_op jit(solution)/shard_map/dot_general | solution.py:61
  144.0 12.8 %copy.9 = f32[768,4096]{1,0:T(8,128)} copy(f32[768,4096]{0,1:T(8,128)} %convolution_bitcast_fusion) | data formatting | bytes 25165824
  156.8 80.6 %all-reduce.3.cloned.1.call-done = (f32[4096,64]{0,1:T(8,128)}, f32[64,4096]{1,0:T(8,128)}) async-done(((f32[4096,64]{0,1:T(8,128)}, f32[64,4096]{1,0:T(8,128)}), (f32[4096,64]{0,1:T(8,128)}, f32[64,4096]{1,0:T(8,128)})) %all-reduce.3.cloned.1.call-update) | async-done | bytes 2097168 | tf_op jit(solution)/shard_map/psum | solution.py:67
  237.4 2.3 copy.12
  239.7 2.3 copy.13
  (29 shorter events, 2.1 us)
Async XLA Ops:
  7.2 83.6 %copy-start = (bf16[64,4096]{1,0:T(8,128)(2,1)S(1)}, bf16[64,4096]{1,0:T(8,128)(2,1)}, u32[]{:S(2)}) copy-start(bf16[64,4096]{1,0:T(8,128)(2,1)} %param.8) | copy-start | bytes 1572868
  7.2 83.3 %copy-start.1 = (bf16[4096,64]{0,1:T(8,128)(2,1)S(1)}, bf16[4096,64]{0,1:T(8,128)(2,1)}, u32[]{:S(2)}) copy-start(bf16[4096,64]{0,1:T(8,128)(2,1)} %param.7) | copy-start | bytes 1572868
  7.2 82.2 %reduce-scatter.2.cloned.1.call-start = ((), (), s32[]{:S(2)}) async-start(), calls=%async_computation.1 | async-start | bytes 4456448 | tf_op jit(solution)/shard_map/reduce_scatter | solution.py:53
  14.1 78.3 %copy-start.3 = (bf16[16,12288]{1,0:T(8,128)(2,1)S(1)}, bf16[16,12288]{1,0:T(8,128)(2,1)}, u32[]{:S(2)}) copy-start(bf16[16,12288]{1,0:T(8,128)(2,1)} %param.9) | copy-start | bytes 1179652
  14.1 121.9 %all-gather.2.cloned.1.call-start = ((), (), s32[]{:S(2)}) async-start(), calls=%async_computation.2 | async-start | bytes 2228224 | tf_op jit(solution)/shard_map/all_gather | solution.py:63
  95.4 142.0 %all-reduce.3.cloned.1.call-start = ((), (), s32[]{:S(2)}) async-start(), calls=%async_computation.3 | async-start | bytes 4194304 | tf_op jit(solution)/shard_map/psum | solution.py:67
  96.1 39.8 %copy-start.2 = (bf16[256,768]{1,0:T(8,128)(2,1)S(1)}, bf16[256,768]{1,0:T(8,128)(2,1)}, u32[]{:S(2)}) copy-start(bf16[256,768]{1,0:T(8,128)(2,1)} %param.5) | copy-start | bytes 1179652
Sparse Core Ops, SparseCore 0:
  14.2 75.1 reduce-scatter.1
  95.5 40.3 all-gather.1
  140.6 96.7 all-reduce.2
where the time goes:
time: 249 us; the launch traced here: 248 us
  waiting for transfers between devices  192 us (77%)
  matrix products  22 us (9%)
  local copies, waits for them, and re-layouts  17.4 us (7%)
  between operations  13.8 us (6%)
  other arithmetic  3.47 us (1%)
    psum x1, waiting for transfers between devices, local(): down_grad, up_grad = lax.psum((down_part, up_part), 'tok')  80.6 us
    reduce_scatter x1, waiting for transfers between devices, local(): lax.psum_scatter(jnp.dot(tap_rows, w_join, preferred_element_type=jnp.flo...  75.2 us
    all_gather x1, waiting for transfers between devices, local(): lax.all_gather(joined_cot, 'tok', axis=0, tiled=True)  35.7 us
    unnamed x11, local copies, waits for them, and re-layouts  17.4 us
    dot_general x1, matrix products, local(): lax.dot_general(tap_rows, lax.all_gather(joined_cot, 'tok', axis=0, tiled...  8.04 us
    dot_general x1, matrix products, local(): jnp.dot(tap_rows, w_join, preferred_element_type=jnp.float32)  6.81 us
  transfers between devices with their start and end apart: 3, of which 3 were waited for; matrix products, arithmetic and copies ran while one was open for 10% of the time, Pallas kernels for 0%

commit v1 on v0

v1 whole, which is shorter than its diff:
```python
import functools

import jax
import jax.numpy as jnp
from jax import lax
from jax.experimental import pallas as pl
from jax.experimental.pallas import tpu as pltpu
from jax.sharding import PartitionSpec as P

STEPS = 3
CHUNKS = 4
GRAD_CHUNKS = 2
ROWS = 16
TILE = 512
MESH = pl.DeviceIdType.MESH
F32 = jnp.float32
BF16 = jnp.bfloat16


def nt_dot(a, b):
    return lax.dot_general(a, b, (((1,), (1,)), ((), ())), preferred_element_type=F32)


def tn_dot(a, b):
    return lax.dot_general(a, b, (((0,), (0,)), ((), ())), preferred_element_type=F32)


def axis_orders(levels):
    first = list(range(levels))
    second = [0, 2, 1] + first[3:] if levels > 2 else first
    return first, second


def block_at(order, position, levels):
    return sum(((position >> (levels - 1 - i)) & 1) << order[i] for i in range(levels))


def exchange_kernel(n, levels, taps_hbm, w_hbm, down_hbm, up_hbm, upstream_hbm,
                    drafts_ref, cot_hbm, tap_rows_ref, grads_ref,
                    taps, w, w_down, w_up, upstream,
                    acc, gather, joined, states, pres, normed, lows, acts, low_cots,
                    partial, grad_acc, grad_gather, *rest):
    out_bufs = rest[0:levels]
    in_bufs = rest[levels:2 * levels]
    grad_out = rest[2 * levels:3 * levels]
    grad_in = rest[3 * levels:4 * levels]
    (rs_send, rs_recv, ag_send, ag_recv, grs_send, grs_recv, gag_send, gag_recv,
     w_sem, small_sem, cot_sem) = rest[4 * levels:]
    me = lax.axis_index("tok")
    bits = [(me // 2 ** b) % 2 for b in range(levels)]
    partners = [me + (1 - 2 * bits[b]) * 2 ** b for b in range(levels)]
    orders = axis_orders(levels)
    chunks, _, _, cw = gather.shape
    hid = chunks * cw
    gcw = grad_gather.shape[3]

    def xor_me(p):
        return sum(((1 - bits[b]) if (p >> b) & 1 else bits[b]) * 2 ** b for b in range(levels))

    taps_copy = pltpu.make_async_copy(taps_hbm, taps, small_sem.at[0])
    taps_copy.start()
    w_copies = [
        pltpu.make_async_copy(w_hbm.at[:, pl.ds(c * cw, cw)], w.at[c], w_sem.at[c])
        for c in range(chunks)
    ]
    for copy in w_copies:
        copy.start()
    small = [
        pltpu.make_async_copy(src, dst, small_sem.at[1 + i])
        for i, (src, dst) in enumerate(((down_hbm, w_down), (up_hbm, w_up), (upstream_hbm, upstream)))
    ]
    for copy in small:
        copy.start()

    barrier = pltpu.get_barrier_semaphore()
    for b in range(levels):
        pl.semaphore_signal(barrier, inc=1, device_id={"tok": partners[b]}, device_id_type=MESH)

    taps_copy.wait()
    for o, order in enumerate(orders):
        for q in range(n):
            tap_rows_ref[o, pl.ds(q * ROWS, ROWS), :] = taps[xor_me(block_at(order, q, levels))]
    pl.semaphore_wait(barrier, levels)

    pending = []

    def remote(src, dst, send, recv, b):
        copy = pltpu.make_async_remote_copy(
            src_ref=src, dst_ref=dst, send_sem=send, recv_sem=recv,
            device_id={"tok": partners[b]}, device_id_type=MESH)
        copy.start()
        pending.append(copy)
        return copy

    half = n // 2
    rs = {}

    def order_of(c):
        return orders[c % 2]

    def rs_stage(i, c, accs, outs, ins, send, recv, table):
        m = n >> i
        h = m // 2
        table[i - 1, c].wait_recv()
        got = ins[i - 1]
        outs[i][c] = (accs[c, h:m] + got[c, h:m].astype(F32)).astype(BF16)
        table[i, c] = remote(outs[i].at[c], ins[i].at[c], send.at[i, c], recv.at[i, c], order_of(c)[i])
        accs[c, 0:h] = accs[c, 0:h] + got[c, 0:h].astype(F32)

    def rs_last(c, accs, ins, table):
        table[levels - 1, c].wait_recv()
        return accs[c, 0] + ins[levels - 1][c, 0].astype(F32)

    def join_stage(i, c):
        if i == 0:
            w_copies[c].wait()
            tw = min(TILE, cw)
            for j in range(cw // tw):
                cols = slice(j * tw, (j + 1) * tw)
                tile = w[c, :, cols]
                away = jnp.dot(tap_rows_ref[c % 2, half * ROWS:, :], tile, preferred_element_type=F32)
                out_bufs[0][c, :, :, cols] = away.astype(BF16).reshape(half, ROWS, tw)
                kept = jnp.dot(tap_rows_ref[c % 2, :half * ROWS, :], tile, preferred_element_type=F32)
                acc[c, :, :, cols] = kept.reshape(half, ROWS, tw)
            rs[0, c] = remote(out_bufs[0].at[c], in_bufs[0].at[c], rs_send.at[0, c], rs_recv.at[0, c],
                              order_of(c)[0])
        elif i < levels:
            rs_stage(i, c, acc, out_bufs, in_bufs, rs_send, rs_recv, rs)
        else:
            joined[:, c * cw:(c + 1) * cw] = rs_last(c, acc, in_bufs, rs).astype(BF16)

    steps = sorted((c + 2 * i, -i, i, c) for i in range(levels + 1) for c in range(chunks))
    for _, _, i, c in steps:
        join_stage(i, c)

    for copy in small:
        copy.wait()

    def inverse_norm(state):
        return lax.rsqrt(jnp.mean(state * state, axis=-1, keepdims=True) + 1e-06)

    state = joined[...].astype(F32)
    invs = []
    for s in range(STEPS):
        states[s] = state
        inv = inverse_norm(state)
        invs.append(inv)
        rows = (state * inv).astype(BF16)
        normed[s * ROWS:(s + 1) * ROWS, :] = rows
        low = jnp.dot(rows, w_down[...], preferred_element_type=F32).astype(BF16)
        lows[s * ROWS:(s + 1) * ROWS, :] = low
        pre = jnp.dot(low, w_up[...], preferred_element_type=F32)
        pres[s] = pre
        state = states[s] + pre * jax.nn.sigmoid(pre)
        drafts_ref[:, s * hid:(s + 1) * hid] = state.astype(BF16)

    g = jnp.zeros((ROWS, hid), F32)
    for s in reversed(range(STEPS)):
        inv = invs[s]
        g = g + upstream[:, s * hid:(s + 1) * hid].astype(F32)
        pre = pres[s]
        sigma = jax.nn.sigmoid(pre)
        act = (g * sigma * (1.0 + pre * (1.0 - sigma))).astype(BF16)
        acts[s * ROWS:(s + 1) * ROWS, :] = act
        low_cot = nt_dot(act, w_up[...]).astype(BF16)
        low_cots[s * ROWS:(s + 1) * ROWS, :] = low_cot
        back = nt_dot(low_cot, w_down[...])
        prior = states[s]
        inner = jnp.mean(back * prior, axis=-1, keepdims=True)
        g = g + back * inv - prior * (inv * inv * inv * inner)
    cot = g.astype(BF16)
    for c in range(chunks):
        gather[c, 0] = cot[:, c * cw:(c + 1) * cw]

    def ag_stage(i, c, buf, send, recv, table):
        m = n >> (i + 1)
        if i < levels - 1:
            table[i + 1, c].wait_recv()
        table[i, c] = remote(buf.at[c, pl.ds(0, m)], buf.at[c, pl.ds(m, m)], send.at[i, c], recv.at[i, c],
                             order_of(c)[i])

    ag, grs, gag = {}, {}, {}
    for c in range(chunks):
        ag_stage(levels - 1, c, gather, ag_send, ag_recv, ag)

    rank = w_up.shape[0]
    blocks = rank // ROWS
    gw = partial.shape[2]
    for j in range(hid // gw):
        cols = slice(j * gw, (j + 1) * gw)
        partial[2 * blocks * j:2 * blocks * j + blocks] = tn_dot(
            low_cots[...], normed[:, cols]).reshape(blocks, ROWS, gw)
        partial[2 * blocks * j + blocks:2 * blocks * (j + 1)] = tn_dot(
            lows[...], acts[:, cols]).reshape(blocks, ROWS, gw)

    def grad_stage(i, c):
        if i == 0:
            for q in range(half, n):
                d = xor_me(block_at(order_of(c), q, levels))
                grad_out[0][c, q - half] = partial[d, :, c * gcw:(c + 1) * gcw].astype(BF16)
            grs[0, c] = remote(grad_out[0].at[c], grad_in[0].at[c], grs_send.at[0, c], grs_recv.at[0, c],
                               order_of(c)[0])
            for q in range(half):
                d = xor_me(block_at(order_of(c), q, levels))
                grad_acc[c, q] = partial[d, :, c * gcw:(c + 1) * gcw]
        elif i < levels:
            rs_stage(i, c, grad_acc, grad_out, grad_in, grs_send, grs_recv, grs)
        else:
            grad_gather[c, 0] = rs_last(c, grad_acc, grad_in, grs).astype(BF16)
            ag_stage(levels - 1, c, grad_gather, gag_send, gag_recv, gag)

    for i in range(levels):
        for c in range(GRAD_CHUNKS):
            grad_stage(i, c)
        if i < levels - 1:
            for c in range(chunks):
                ag_stage(levels - 2 - i, c, gather, ag_send, ag_recv, ag)
    for c in range(GRAD_CHUNKS):
        grad_stage(levels, c)
    cot_copies = []
    for c in range(chunks):
        ag[0, c].wait_recv()
        copy = pltpu.make_async_copy(gather.at[c], cot_hbm.at[c], cot_sem.at[c])
        copy.start()
        cot_copies.append(copy)
    for i in reversed(range(levels - 1)):
        for c in range(GRAD_CHUNKS):
            ag_stage(i, c, grad_gather, gag_send, gag_recv, gag)
    for c in range(GRAD_CHUNKS):
        gag[0, c].wait_recv()
        for q in range(n):
            d = xor_me(block_at(order_of(c), q, levels))
            rows = pl.multiple_of((d % (2 * blocks)) * ROWS, ROWS)
            cols = pl.multiple_of((d // (2 * blocks)) * gw + c * gcw, 128)
            grads_ref[pl.ds(rows, ROWS), pl.ds(cols, gcw)] = grad_gather[c, q]
    for copy in pending:
        copy.wait_send()
    for copy in cot_copies:
        copy.wait()


def join_grad_kernel(rows_ref, cot_ref, grads_ref, out_ref, down_ref, up_ref):
    c = pl.program_id(0)
    out_ref[...] = tn_dot(rows_ref[c % 2], cot_ref[0])
    rank = up_ref.shape[0]
    grads = grads_ref[...].astype(F32)
    down_ref[...] = grads[:rank].T
    up_ref[...] = grads[rank:]


def local(n, taps, w_join, w_down, w_up, upstream):
    levels = n.bit_length() - 1
    tokens, features = taps.shape
    hid = w_join.shape[1]
    rank = w_up.shape[0]
    cw = hid // CHUNKS
    gw = 2 * rank * hid // (ROWS * n)
    gcw = gw // GRAD_CHUNKS
    half = n // 2
    any_spec = pl.BlockSpec(memory_space=pl.ANY)
    vmem_spec = pl.BlockSpec(memory_space=pltpu.VMEM)
    halves = [pltpu.VMEM((CHUNKS, n >> (i + 1), ROWS, cw), BF16) for i in range(levels)]
    grad_halves = [pltpu.VMEM((GRAD_CHUNKS, n >> (i + 1), ROWS, gcw), BF16) for i in range(levels)]
    dma = pltpu.SemaphoreType.DMA
    drafts, cot, tap_rows, grads = pl.pallas_call(
        functools.partial(exchange_kernel, n, levels),
        out_shape=(
            jax.ShapeDtypeStruct((ROWS, STEPS * hid), BF16),
            jax.ShapeDtypeStruct((CHUNKS, n, ROWS, cw), BF16),
            jax.ShapeDtypeStruct((2, tokens, features), BF16),
            jax.ShapeDtypeStruct((2 * rank, hid), BF16),
        ),
        in_specs=[any_spec] * 5,
        out_specs=(vmem_spec, any_spec, vmem_spec, vmem_spec),
        scratch_shapes=[
            pltpu.VMEM((n, ROWS, features), BF16),
            pltpu.VMEM((CHUNKS, features, cw), BF16),
            pltpu.VMEM((hid, rank), BF16),
            pltpu.VMEM((rank, hid), BF16),
            pltpu.VMEM((ROWS, STEPS * hid), BF16),
            pltpu.VMEM((CHUNKS, half, ROWS, cw), F32),
            pltpu.VMEM((CHUNKS, n, ROWS, cw), BF16),
            pltpu.VMEM((ROWS, hid), BF16),
            pltpu.VMEM((STEPS, ROWS, hid), F32),
            pltpu.VMEM((STEPS, ROWS, hid), F32),
            pltpu.VMEM((STEPS * ROWS, hid), BF16),
            pltpu.VMEM((STEPS * ROWS, rank), BF16),
            pltpu.VMEM((STEPS * ROWS, hid), BF16),
            pltpu.VMEM((STEPS * ROWS, rank), BF16),
            pltpu.VMEM((n, ROWS, gw), F32),
            pltpu.VMEM((GRAD_CHUNKS, half, ROWS, gcw), F32),
            pltpu.VMEM((GRAD_CHUNKS, n, ROWS, gcw), BF16),
            *halves, *halves, *grad_halves, *grad_halves,
            *[dma((levels, CHUNKS))] * 4,
            *[dma((levels, GRAD_CHUNKS))] * 4,
            dma((CHUNKS,)),
            dma((4,)),
            dma((CHUNKS,)),
        ],
        compiler_params=pltpu.CompilerParams(
            collective_id=0, has_side_effects=True, vmem_limit_bytes=60 * 1024 * 1024),
    )(taps.reshape(n, ROWS, features), w_join, w_down, w_up, upstream)
    tw = min(TILE, cw)
    per = cw // tw
    join_grad, down_grad, up_grad = pl.pallas_call(
        join_grad_kernel,
        grid=(CHUNKS, per),
        out_shape=(
            jax.ShapeDtypeStruct((features, hid), F32),
            jax.ShapeDtypeStruct((hid, rank), F32),
            jax.ShapeDtypeStruct((rank, hid), F32),
        ),
        in_specs=[
            pl.BlockSpec((2, tokens, features), lambda c, j: (0, 0, 0)),
            pl.BlockSpec((1, tokens, tw), lambda c, j: (c, 0, j)),
            pl.BlockSpec((2 * rank, tw), lambda c, j: (0, c * per + j)),
        ],
        out_specs=(
            pl.BlockSpec((features, tw), lambda c, j: (0, c * per + j)),
            pl.BlockSpec((tw, rank), lambda c, j: (c * per + j, 0)),
            pl.BlockSpec((rank, tw), lambda c, j: (0, c * per + j)),
        ),
        compiler_params=pltpu.CompilerParams(vmem_limit_bytes=48 * 1024 * 1024),
    )(tap_rows, cot.reshape(CHUNKS, tokens, cw), grads)
    return drafts, join_grad, down_grad, up_grad


def solution(mesh):
    in_specs = (P("groups", "tok"), P("tok", None), P(), P(), P(("groups", "tok"), None))
    out_specs = (
        P(("groups", "tok"), None),
        P("tok", "groups"),
        P("groups", None),
        P("groups", None),
    )
    return jax.shard_map(
        functools.partial(local, mesh.shape["tok"]), mesh=mesh, in_specs=in_specs, out_specs=out_specs,
        check_vma=False)
```

time: 249 us -> 81.3 us (0.33)
  waiting for transfers between devices: 192 us -> 0 us
  Pallas kernels: 0 us -> 71.7 us
  matrix products: 22 us -> 0 us
  between operations: 13.8 us -> 0.65 us
  local copies, waits for them, and re-layouts: 17.4 us -> 8.61 us
  other arithmetic: 3.47 us -> 0 us
    psum x1 -> x0, waiting for transfers between devices: 80.6 us -> none  [local(): down_grad, up_grad = lax.psum((down_part, up_part), 'tok')]
    reduce_scatter x1 -> x0, waiting for transfers between devices: 75.2 us -> none  [local(): lax.psum_scatter(jnp.dot(tap_rows, w_join, preferred_element_type=jnp.flo...]
    pallas_call x0 -> x2, Pallas kernels: none -> 71.7 us  [the longest x1 64.9 us: local(): pl.pallas_call(functools.partial(exchange_kernel, n, levels), out_shape=(...]
    all_gather x1 -> x0, waiting for transfers between devices: 35.7 us -> none  [local(): lax.all_gather(joined_cot, 'tok', axis=0, tiled=True)]
    dot_general x20 -> x0, matrix products: 22 us -> none  [the longest x1 8.04 us: local(): lax.dot_general(tap_rows, lax.all_gather(joined_cot, 'tok', axis=0, tiled...]
    unnamed x11, local copies, waits for them, and re-layouts: 17.4 us -> 8.61 us
  transfers between devices with their start and end apart: 3 -> 0, of which waited for: 3 -> 0; matrix products, arithmetic and copies ran while one was open for 10% -> 0% of each run, Pallas kernels for 0% -> 0%
where the time goes in v1:
time: 81.3 us; the launch traced here: 81 us
  Pallas kernels  71.7 us (88%)
  local copies, waits for them, and re-layouts  8.61 us (11%)
    pallas_call x1, Pallas kernels, local(): pl.pallas_call(functools.partial(exchange_kernel, n, levels), out_shape=(...  64.9 us
    unnamed x11, local copies, waits for them, and re-layouts  8.61 us
    pallas_call x1, Pallas kernels, local(): pl.pallas_call(join_grad_kernel, grid=(CHUNKS, per), out_shape=(jax.Shape...  6.87 us

profile of v1, /device:TPU:0, one launch (start us, length us, event | category | flops | bytes accessed | tf_op | source)
XLA Modules:
  0.0 81.0 jit_solution(11813097897504889974)
XLA Ops:
  0.6 2.4 %copy.9.down_hbm = bf16[4096,64]{1,0:T(8,128)(2,1)} copy(bf16[4096,64]{0,1:T(8,128)(2,1)} %param.7) | data formatting | bytes 1048576 | tf_op args[2]
  3.0 64.9 %shard_map.84 = (bf16[16,12288]{1,0:T(8,128)(2,1)}, bf16[4,16,16,1024]{3,2,1,0:T(8,128)(2,1)}, bf16[2,256,768]{2,1,0:T(8,128)(2,1)}, bf16[128,4096]{1,0:T(8,128)(2,1)}) custom-call(bf16[16,16,768]{2,1,0:T(8,128)(2,1)} %bitcast.3, bf16[768,4096]{1,0:T(8,128)(2,1)} %w_hbm.1, bf16[4096,64]{1,0:T(8,128)(2,1)} %copy.9.down_hbm, bf16[64,4096]{1,0:T(8,128)(2,1)} %up_hbm.1, ...), custom_call_target="tpu_custom_call" | custom-call | tf_op jit(solution)/shard_map/pallas_call | solution.py:265
  67.9 0.0 copy-start
  67.9 1.6 %copy-done = bf16[4,16,16,1024]{3,2,1,0:T(8,128)(2,1)S(1)} copy-done((bf16[4,16,16,1024]{3,2,1,0:T(8,128)(2,1)S(1)}, bf16[4,16,16,1024]{3,2,1,0:T(8,128)(2,1)}, u32[]{:S(2)}) %copy-start) | copy-done | bytes 2097176
  69.5 0.0 copy-start.1
  69.5 1.2 %copy-done.1 = bf16[128,4096]{1,0:T(8,128)(2,1)S(1)} copy-done((bf16[128,4096]{1,0:T(8,128)(2,1)S(1)}, bf16[128,4096]{1,0:T(8,128)(2,1)}, u32[]{:S(2)}) %copy-start.1) | copy-done | bytes 1048600
  70.7 0.0 copy-start.2
  70.7 1.1 %copy-done.2 = bf16[2,256,768]{2,1,0:T(8,128)(2,1)S(1)} copy-done((bf16[2,256,768]{2,1,0:T(8,128)(2,1)S(1)}, bf16[2,256,768]{2,1,0:T(8,128)(2,1)}, u32[]{:S(2)}) %copy-start.2) | copy-done | bytes 786456
  71.8 0.0 copy-start.3
  71.8 6.9 %shard_map.85 = (f32[768,4096]{1,0:T(8,128)}, f32[4096,64]{1,0:T(8,128)S(1)}, f32[64,4096]{1,0:T(8,128)}) custom-call(bf16[2,256,768]{2,1,0:T(8,128)(2,1)S(1)} %copy-done.2, bf16[4,256,1024]{2,1,0:T(8,128)(2,1)S(1)} %bitcast.2, bf16[128,4096]{1,0:T(8,128)(2,1)S(1)} %copy-done.1), custom_call_target="tpu_custom_call" | custom-call | tf_op jit(solution)/shard_map/pallas_call | solution.py:305
  78.7 1.6 %copy.10 = f32[4096,64]{0,1:T(8,128)} copy(f32[4096,64]{1,0:T(8,128)S(1)} %get-tuple-element.20) | data formatting | bytes 2097152
  80.2 0.0 copy-done.3
  80.2 0.7 copy.12
Async XLA Ops:
  67.9 1.6 %copy-start = (bf16[4,16,16,1024]{3,2,1,0:T(8,128)(2,1)S(1)}, bf16[4,16,16,1024]{3,2,1,0:T(8,128)(2,1)}, u32[]{:S(2)}) copy-start(bf16[4,16,16,1024]{3,2,1,0:T(8,128)(2,1)} %get-tuple-element.13) | copy-start | bytes 6291460
  69.5 1.2 %copy-start.1 = (bf16[128,4096]{1,0:T(8,128)(2,1)S(1)}, bf16[128,4096]{1,0:T(8,128)(2,1)}, u32[]{:S(2)}) copy-start(bf16[128,4096]{1,0:T(8,128)(2,1)} %get-tuple-element.14.grads_ref) | copy-start | bytes 3145732
  70.7 1.1 %copy-start.2 = (bf16[2,256,768]{2,1,0:T(8,128)(2,1)S(1)}, bf16[2,256,768]{2,1,0:T(8,128)(2,1)}, u32[]{:S(2)}) copy-start(bf16[2,256,768]{2,1,0:T(8,128)(2,1)} %get-tuple-element.12.rows_ref) | copy-start | bytes 2359300
  71.8 8.4 %copy-start.3 = (bf16[16,12288]{1,0:T(8,128)(2,1)S(1)}, bf16[16,12288]{1,0:T(8,128)(2,1)}, u32[]{:S(2)}) copy-start(bf16[16,12288]{1,0:T(8,128)(2,1)} %get-tuple-element.26) | copy-start | bytes 1179652

commit v2 on v1

--- a/solution.py
+++ b/solution.py
@@ -11,7 +11,10 @@
 CHUNKS = 4
 GRAD_CHUNKS = 2
 ROWS = 16
-TILE = 512
+JOIN_LAG = 8
+COT_PACE = (0.01, 3.2)
+GRAD_PACE = (0.01, 1.6)
+TILE = 1024
 MESH = pl.DeviceIdType.MESH
 F32 = jnp.float32
 BF16 = jnp.bfloat16
@@ -23,6 +26,10 @@
 
 def tn_dot(a, b):
     return lax.dot_general(a, b, (((0,), (0,)), ((), ())), preferred_element_type=F32)
+
+
+def order_index(c):
+    return c % 2
 
 
 def axis_orders(levels):
@@ -36,8 +43,8 @@
 
 
 def exchange_kernel(n, levels, taps_hbm, w_hbm, down_hbm, up_hbm, upstream_hbm,
-                    drafts_ref, cot_hbm, tap_rows_ref, grads_ref,
-                    taps, w, w_down, w_up, upstream,
+                    drafts_ref, cot_hbm, taps_t_ref, grads_ref,
+                    taps, tap_rows, w, w_down, w_up, upstream,
                     acc, gather, joined, states, pres, normed, lows, acts, low_cots,
                     partial, grad_acc, grad_gather, *rest):
     out_bufs = rest[0:levels]
@@ -79,7 +86,7 @@
     taps_copy.wait()
     for o, order in enumerate(orders):
         for q in range(n):
-            tap_rows_ref[o, pl.ds(q * ROWS, ROWS), :] = taps[xor_me(block_at(order, q, levels))]
+            tap_rows[o, pl.ds(q * ROWS, ROWS), :] = taps[xor_me(block_at(order, q, levels))]
     pl.semaphore_wait(barrier, levels)
 
     pending = []
@@ -96,7 +103,7 @@
     rs = {}
 
     def order_of(c):
-        return orders[c % 2]
+        return orders[order_index(c)]
 
     def rs_stage(i, c, accs, outs, ins, send, recv, table):
         m = n >> i
@@ -114,13 +121,13 @@
     def join_stage(i, c):
         if i == 0:
             w_copies[c].wait()
-            tw = min(TILE, cw)
+            tw = min(512, cw)
             for j in range(cw // tw):
                 cols = slice(j * tw, (j + 1) * tw)
                 tile = w[c, :, cols]
-                away = jnp.dot(tap_rows_ref[c % 2, half * ROWS:, :], tile, preferred_element_type=F32)
+                away = jnp.dot(tap_rows[order_index(c), half * ROWS:, :], tile, preferred_element_type=F32)
                 out_bufs[0][c, :, :, cols] = away.astype(BF16).reshape(half, ROWS, tw)
-                kept = jnp.dot(tap_rows_ref[c % 2, :half * ROWS, :], tile, preferred_element_type=F32)
+                kept = jnp.dot(tap_rows[order_index(c), :half * ROWS, :], tile, preferred_element_type=F32)
                 acc[c, :, :, cols] = kept.reshape(half, ROWS, tw)
             rs[0, c] = remote(out_bufs[0].at[c], in_bufs[0].at[c], rs_send.at[0, c], rs_recv.at[0, c],
                               order_of(c)[0])
@@ -129,8 +136,11 @@
         else:
             joined[:, c * cw:(c + 1) * cw] = rs_last(c, acc, in_bufs, rs).astype(BF16)
 
-    steps = sorted((c + 2 * i, -i, i, c) for i in range(levels + 1) for c in range(chunks))
-    for _, _, i, c in steps:
+    steps = sorted((c + JOIN_LAG * i, -i, i, c) for i in range(levels + 1) for c in range(chunks))
+    for at, (_, _, i, c) in enumerate(steps):
+        if at == 2 * chunks:
+            for o in range(2):
+                taps_t_ref[o] = tap_rows[o].T
         join_stage(i, c)
 
     for copy in small:
@@ -147,7 +157,7 @@
         invs.append(inv)
         rows = (state * inv).astype(BF16)
         normed[s * ROWS:(s + 1) * ROWS, :] = rows
-        low = jnp.dot(rows, w_down[...], preferred_element_type=F32).astype(BF16)
+        low = nt_dot(rows, w_down[...]).astype(BF16)
         lows[s * ROWS:(s + 1) * ROWS, :] = low
         pre = jnp.dot(low, w_up[...], preferred_element_type=F32)
         pres[s] = pre
@@ -164,7 +174,7 @@
         acts[s * ROWS:(s + 1) * ROWS, :] = act
         low_cot = nt_dot(act, w_up[...]).astype(BF16)
         low_cots[s * ROWS:(s + 1) * ROWS, :] = low_cot
-        back = nt_dot(low_cot, w_down[...])
+        back = jnp.dot(low_cot, w_down[...], preferred_element_type=F32)
         prior = states[s]
         inner = jnp.mean(back * prior, axis=-1, keepdims=True)
         g = g + back * inv - prior * (inv * inv * inv * inner)
@@ -209,23 +219,27 @@
             grad_gather[c, 0] = rs_last(c, grad_acc, grad_in, grs).astype(BF16)
             ag_stage(levels - 1, c, grad_gather, gag_send, gag_recv, gag)
 
-    for i in range(levels):
-        for c in range(GRAD_CHUNKS):
-            grad_stage(i, c)
-        if i < levels - 1:
-            for c in range(chunks):
-                ag_stage(levels - 2 - i, c, gather, ag_send, ag_recv, ag)
-    for c in range(GRAD_CHUNKS):
-        grad_stage(levels, c)
     cot_copies = []
-    for c in range(chunks):
-        ag[0, c].wait_recv()
-        copy = pltpu.make_async_copy(gather.at[c], cot_hbm.at[c], cot_sem.at[c])
-        copy.start()
-        cot_copies.append(copy)
-    for i in reversed(range(levels - 1)):
-        for c in range(GRAD_CHUNKS):
-            ag_stage(i, c, grad_gather, gag_send, gag_recv, gag)
+
+    def cot_stage(k, c):
+        if k < levels:
+            ag_stage(levels - 1 - k, c, gather, ag_send, ag_recv, ag)
+        else:
+            ag[0, c].wait_recv()
+            copy = pltpu.make_async_copy(gather.at[c], cot_hbm.at[c], cot_sem.at[c])
+            copy.start()
+            cot_copies.append(copy)
+
+    def grad_step(k, c):
+        if k <= levels:
+            grad_stage(k, c)
+        elif k < 2 * levels:
+            ag_stage(2 * levels - 1 - k, c, grad_gather, gag_send, gag_recv, gag)
+
+    events = [(COT_PACE[0] * c + COT_PACE[1] * k, 1, k, c) for k in range(1, levels + 1) for c in range(chunks)]
+    events += [(GRAD_PACE[0] * c + GRAD_PACE[1] * k, 0, k, c) for k in range(2 * levels) for c in range(GRAD_CHUNKS)]
+    for _, kind, k, c in sorted(events):
+        (cot_stage if kind else grad_step)(k, c)
     for c in range(GRAD_CHUNKS):
         gag[0, c].wait_recv()
         for q in range(n):
@@ -239,12 +253,13 @@
         copy.wait()
 
 
-def join_grad_kernel(rows_ref, cot_ref, grads_ref, out_ref, down_ref, up_ref):
+def join_grad_kernel(rows_ref, cot_ref, grads_ref, drafts_ref, out_ref, down_ref, up_ref, drafts_out_ref):
+    drafts_out_ref[...] = drafts_ref[...]
     c = pl.program_id(0)
-    out_ref[...] = tn_dot(rows_ref[c % 2], cot_ref[0])
+    out_ref[...] = jnp.dot(rows_ref[order_index(c)], cot_ref[0], preferred_element_type=F32)
     rank = up_ref.shape[0]
     grads = grads_ref[...].astype(F32)
-    down_ref[...] = grads[:rank].T
+    down_ref[...] = grads[:rank]
     up_ref[...] = grads[rank:]
 
 
@@ -267,15 +282,16 @@
         out_shape=(
             jax.ShapeDtypeStruct((ROWS, STEPS * hid), BF16),
             jax.ShapeDtypeStruct((CHUNKS, n, ROWS, cw), BF16),
-            jax.ShapeDtypeStruct((2, tokens, features), BF16),
+            jax.ShapeDtypeStruct((2, features, tokens), BF16),
             jax.ShapeDtypeStruct((2 * rank, hid), BF16),
         ),
         in_specs=[any_spec] * 5,
         out_specs=(vmem_spec, any_spec, vmem_spec, vmem_spec),
         scratch_shapes=[
             pltpu.VMEM((n, ROWS, features), BF16),
+            pltpu.VMEM((2, tokens, features), BF16),
             pltpu.VMEM((CHUNKS, features, cw), BF16),
-            pltpu.VMEM((hid, rank), BF16),
+            pltpu.VMEM((rank, hid), BF16),
             pltpu.VMEM((rank, hid), BF16),
             pltpu.VMEM((ROWS, STEPS * hid), BF16),
             pltpu.VMEM((CHUNKS, half, ROWS, cw), F32),
@@ -299,30 +315,34 @@
         ],
         compiler_params=pltpu.CompilerParams(
             collective_id=0, has_side_effects=True, vmem_limit_bytes=60 * 1024 * 1024),
-    )(taps.reshape(n, ROWS, features), w_join, w_down, w_up, upstream)
+    )(taps.reshape(n, ROWS, features), w_join, w_down.T, w_up, upstream)
     tw = min(TILE, cw)
     per = cw // tw
-    join_grad, down_grad, up_grad = pl.pallas_call(
+    dw = STEPS * hid // (CHUNKS * per)
+    join_grad, down_grad, up_grad, drafts = pl.pallas_call(
         join_grad_kernel,
         grid=(CHUNKS, per),
         out_shape=(
             jax.ShapeDtypeStruct((features, hid), F32),
-            jax.ShapeDtypeStruct((hid, rank), F32),
             jax.ShapeDtypeStruct((rank, hid), F32),
+            jax.ShapeDtypeStruct((rank, hid), F32),
+            jax.ShapeDtypeStruct((ROWS, STEPS * hid), BF16),
         ),
         in_specs=[
-            pl.BlockSpec((2, tokens, features), lambda c, j: (0, 0, 0)),
+            pl.BlockSpec((2, features, tokens), lambda c, j: (0, 0, 0)),
             pl.BlockSpec((1, tokens, tw), lambda c, j: (c, 0, j)),
             pl.BlockSpec((2 * rank, tw), lambda c, j: (0, c * per + j)),
+            pl.BlockSpec((ROWS, dw), lambda c, j: (0, c * per + j)),
         ],
         out_specs=(
             pl.BlockSpec((features, tw), lambda c, j: (0, c * per + j)),
-            pl.BlockSpec((tw, rank), lambda c, j: (c * per + j, 0)),
             pl.BlockSpec((rank, tw), lambda c, j: (0, c * per + j)),
+            pl.BlockSpec((rank, tw), lambda c, j: (0, c * per + j)),
+            pl.BlockSpec((ROWS, dw), lambda c, j: (0, c * per + j)),
         ),
-        compiler_params=pltpu.CompilerParams(vmem_limit_bytes=48 * 1024 * 1024),
-    )(tap_rows, cot.reshape(CHUNKS, tokens, cw), grads)
-    return drafts, join_grad, down_grad, up_grad
+        compiler_params=pltpu.CompilerParams(vmem_limit_bytes=60 * 1024 * 1024),
+    )(tap_rows, cot.reshape(CHUNKS, tokens, cw), grads, drafts)
+    return drafts, join_grad, down_grad.T, up_grad
 
 
 def solution(mesh):

time: 81.3 us -> 68.8 us (0.85)
  local copies, waits for them, and re-layouts: 8.61 us -> 0 us
  Pallas kernels: 71.7 us -> 67.4 us
    unnamed x11 -> x0, local copies, waits for them, and re-layouts: 8.61 us -> none
    pallas_call x1, Pallas kernels: 64.9 us -> 59.4 us  [local(): pl.pallas_call(functools.partial(exchange_kernel, n, levels), out_shape=(...]
    pallas_call x1, Pallas kernels: 6.87 us -> 8.02 us  [local(): pl.pallas_call(join_grad_kernel, grid=(CHUNKS, per), out_shape=(jax.Shape...]
where the time goes in v2:
time: 68.8 us; the launch traced here: 68.1 us
  Pallas kernels  67.4 us (98%)
    pallas_call x1, Pallas kernels, local(): pl.pallas_call(functools.partial(exchange_kernel, n, levels), out_shape=(...  59.4 us
    pallas_call x1, Pallas kernels, local(): pl.pallas_call(join_grad_kernel, grid=(CHUNKS, per), out_shape=(jax.Shape...  8.02 us

profile of v2, /device:TPU:0, one launch (start us, length us, event | category | flops | bytes accessed | tf_op | source)
XLA Modules:
  0.0 68.1 jit_solution(7728080675254397695)
XLA Ops:
  0.6 59.4 %shard_map.84 = (bf16[16,12288]{1,0:T(8,128)(2,1)}, bf16[4,16,16,1024]{3,2,1,0:T(8,128)(2,1)}, bf16[2,768,256]{2,1,0:T(8,128)(2,1)}, bf16[128,4096]{1,0:T(8,128)(2,1)}) custom-call(bf16[16,16,768]{2,1,0:T(8,128)(2,1)} %bitcast.6, bf16[768,4096]{1,0:T(8,128)(2,1)} %w_hbm.1, bf16[64,4096]{1,0:T(8,128)(2,1)} %bitcast.5, bf16[64,4096]{1,0:T(8,128)(2,1)} %up_hbm.1, ...), custom_call_target="tpu_custom_call" | custom-call | tf_op jit(solution)/shard_map/pallas_call | solution.py:280
  60.0 8.0 %shard_map.85 = (f32[768,4096]{1,0:T(8,128)}, f32[64,4096]{1,0:T(8,128)}, f32[64,4096]{1,0:T(8,128)}, bf16[16,12288]{1,0:T(8,128)(2,1)}) custom-call(bf16[2,768,256]{2,1,0:T(8,128)(2,1)} %get-tuple-element.12.rows_ref, bf16[4,256,1024]{2,1,0:T(8,128)(2,1)} %bitcast.4, bf16[128,4096]{1,0:T(8,128)(2,1)} %get-tuple-element.14.grads_ref, ...), custom_call_target="tpu_custom_call" | custom-call | tf_op jit(solution)/shard_map/pallas_call | solution.py:322
